TPU v7x, 256 devices: a whole 4x4x8 slice. The times are simulated.
256 devices in a mesh: batch: 8 (over x, core), slab: 32 (over y, z).
Axes of the slice: x: 4, y: 4, z: 8, core: 2. Of those that a mesh axis runs over, the one named last changes fastest.
Arguments:
- volume: bfloat16 [8, 32, 128, 16, 128], P('batch', None, 'slab'), may hold values from -6 to 6
- kernel: bfloat16 [32, 32, 3, 3, 3], replicated, may hold values from -0.21875 to 0.21875
- offset: float32 [32], replicated, may hold values from -1 to 1
- upstream: bfloat16 [8, 32, 128, 16, 128], P('batch', None, 'slab'), may hold values from -6 to 6
Outputs:
- activated: bfloat16 [8, 32, 128, 16, 128], P('batch', None, 'slab')
- grad_volume: bfloat16 [8, 32, 128, 16, 128], P('batch', None, 'slab')
- grad_kernel: float32 [32, 32, 3, 3, 3], replicated
- grad_offset: float32 [32], replicated
All inputs are finite; a program needn't handle non-finite values.
Results may differ from a plain program's by a relative error of at most 0.0085.
Values may be sent and summed in bfloat16 or wider, within the bound.
A program may use at most 64 MiB of HBM per device.

v0:
```python
import jax
import jax.numpy as jnp
from jax import lax
from jax.sharding import PartitionSpec as P


def padded_2(block, sides, width):
    for axis, dim in sides:
        count = lax.axis_size(axis)
        forward = [(i, i + 1) for i in range(count - 1)]
        backward = [(target, source) for source, target in forward]
        low = lax.ppermute(
            lax.slice_in_dim(block, block.shape[dim] - width, None, axis=dim), axis, forward
        )
        high = lax.ppermute(lax.slice_in_dim(block, 0, width, axis=dim), axis, backward)
        block = jnp.concatenate([low, block, high], axis=dim)
    return block


def convolve_depth(field, weights):
    return lax.conv_general_dilated(
        field,
        weights,
        (1, 1, 1),
        ((0, 0), (1, 1), (1, 1)),
        dimension_numbers=("NCDHW", "OIDHW", "NCDHW"),
        preferred_element_type=jnp.float32,
    )


def pre_gradient(preact, cotangent):
    sig = jax.nn.sigmoid(preact)
    output = (preact * sig).astype(jnp.bfloat16)
    grad_pre = (cotangent.astype(jnp.float32) * sig * (1.0 + preact * (1.0 - sig))).astype(
        jnp.bfloat16
    )
    return (output, grad_pre)


def kernel_terms(haloed, grad_pre, planes):
    rows, cols = (grad_pre.shape[3], grad_pre.shape[4])
    padded = jnp.pad(haloed, ((0, 0), (0, 0), (0, 0), (1, 1), (1, 1)))
    terms = []
    for first in range(3):
        for second in range(3):
            for third in range(3):
                window = padded[
                    :, :, first : first + planes, second : second + rows, third : third + cols
                ]
                terms.append(
                    jnp.einsum(
                        "nodhw,nidhw->oi", grad_pre, window, preferred_element_type=jnp.float32
                    )
                )
    return jnp.stack(terms, axis=2)


def on_device(volume, kernel, offset, upstream):
    planes = volume.shape[2]
    flipped = jnp.transpose(jnp.flip(kernel, (2, 3, 4)), (1, 0, 2, 3, 4))
    bias = offset[None, :, None, None, None]
    haloed = padded_2(volume, (("slab", 2),), 1)
    preact = convolve_depth(haloed, kernel) + bias
    activated, grad_pre = pre_gradient(preact, upstream)
    grad_haloed = padded_2(grad_pre, (("slab", 2),), 1)
    grad_volume = convolve_depth(grad_haloed, flipped).astype(jnp.bfloat16)
    local_kernel = kernel_terms(haloed, grad_pre, planes).reshape(kernel.shape)
    local_offset = jnp.sum(grad_pre.astype(jnp.float32), axis=(0, 2, 3, 4))
    summed_kernel, summed_offset = lax.psum((local_kernel, local_offset), ("batch", "slab"))
    cells = (
        volume.shape[0]
        * planes
        * volume.shape[3]
        * volume.shape[4]
        * lax.axis_size("batch")
        * lax.axis_size("slab")
    )
    scale = 1.0 / jnp.sqrt(jnp.float32(cells))
    return (activated, grad_volume, summed_kernel * scale, summed_offset * scale)


def solution(mesh):
    placed = (P("batch", None, "slab", None, None), P(), P(), P("batch", None, "slab", None, None))
    return jax.shard_map(
        on_device,
        mesh=mesh,
        in_specs=placed,
        out_specs=(
            P("batch", None, "slab", None, None),
            P("batch", None, "slab", None, None),
            P(),
            P(),
        ),
        check_vma=False,
    )
```

profile of v0, /device:TPU:1, one launch (start us, length us, event | category | flops | bytes accessed | tf_op | source)
XLA Modules:
  0.0 333.9 jit_solution(11143610916050945041)
XLA Ops:
  7.2 0.0 all-reduce.3.cloned.1.call-start
  7.2 1.4 copy.135
  8.7 4.4 %collective-permute-start = (bf16[1,32,1,16,128]{4,1,3,2,0:T(8,128)(2,1)S(1)}, bf16[1,32,1,16,128]{4,1,3,2,0:T(8,128)(2,1)S(1)}, u32[]{:S(2)}, u32[]{:S(2)}) collective-permute-start(bf16[1,32,1,16,128]{4,1,3,2,0:T(8,128)(2,1)S(1)} %get-tuple-element.24), channel_id=1, source_target_pairs={{0,1},{1,2},{2,3},{3,4},{4,5},{5,6},{6,7},{7,8},{8,9},{9,10},{10,1... | collective-permute-start | bytes 393224 | tf_op jit(solution)/shard_map/ppermute | solution.py:12
  13.1 1.3 collective-permute-start.1
  14.4 3.2 copy.142
  17.6 1.5 constant_dynamic-update-slice_fusion.1
  19.1 0.3 collective-permute-done.1
  19.4 3.4 %copy.207 = bf16[32,6,16,1,128]{0,2,4,1,3:T(8,128)(2,1)} copy(bf16[32,6,16,1,128]{4,0,2,1,3:T(8,128)(2,1)S(1)} %bitcast.363) | data formatting | bytes 1572864
  22.8 2.5 pad.5.clone
  25.4 0.9 copy.140
  26.3 0.1 slice.134
  26.4 8.8 %add_divide_fusion = (f32[4,16,8,17,32]{4,2,3,1,0:T(8,128)S(1)}, bf16[4,16,8,17,32]{4,2,3,1,0:T(8,128)(2,1)S(1)}, f32[4,16,8,17,32]{4,2,3,1,0:T(8,128)S(1)}) fusion(f32[32]{0:T(128)S(1)} %copy-done.10, pred[8,17]{0,1:T(8,128)(4,1)S(1)} %copy-done.11, bf16[32,32,3,3,3]{1,0,4,3,2:T(8,128)(2,1)S(1)} %copy-done, bf16[32,6,16,1,7,2]{0,4,5,2,1,3:T(8,128)(2,1)S(1)} %slice.134, ...), kind=kOutput, calls=%fused_computation.30 | convolution fusion | flops 466829312 | bytes 3762440 | tf_op jit(solution)/shard_map/conv_general_dilated | solution.py:21
  35.3 0.4 copy.141
  35.6 1.7 slice_bitcast_fusion.3
  37.3 0.8 copy.144
  38.1 1.0 copy.143
  39.1 1.3 convert_reduce_fusion
  40.4 0.2 fusion.138
  40.6 1.1 copy-done.1
  41.7 2.8 copy.148
  44.6 0.4 fusion.49
  44.9 0.3 fusion.48
  45.2 0.4 fusion.47
  45.6 0.4 fusion.46
  45.9 0.3 fusion.45
  46.2 0.4 fusion.44
  46.6 0.4 fusion.43
  46.9 0.3 fusion.42
  47.2 0.4 fusion.41
  47.6 0.4 fusion.40
  47.9 0.3 fusion.39
  48.2 0.4 fusion.38
  48.6 0.4 fusion.37
  49.0 0.5 fusion.36
  49.4 0.4 fusion.35
  49.8 0.4 fusion.34
  50.1 0.3 fusion.33
  50.4 0.4 fusion.32
  50.8 0.4 fusion.31
  51.2 0.3 fusion.30
  51.4 0.4 fusion.29
  51.8 0.4 fusion.28
  52.2 0.3 fusion.27
  52.4 0.4 fusion.26
  52.8 0.4 fusion.25
  53.2 0.3 fusion.24
  53.4 0.4 fusion.23
  53.8 0.8 copy-done.5
  54.6 0.0 all-reduce.3.cloned.1.call-update
  54.6 81.2 %psum.15 = f32[32]{0:T(128)S(1)} all-reduce(f32[32]{0:T(128)S(1)} %get-tuple-element.16), channel_id=1, replica_groups=mesh['batch'=8,'slab'=32] {'batch','slab'}, use_global_device_ids=true, to_apply=%region_2.3 | all-reduce | flops 32 | bytes 256 | tf_op jit(solution)/shard_map/psum | solution.py:69
  135.8 0.5 broadcast_multiply_fusion.1
  136.3 4.0 %copy.178 = bf16[1,32,4,16,128]{4,3,2,1,0:T(8,128)(2,1)} copy(bf16[1,32,4,16,128]{1,3,4,2,0:T(8,128)(2,1)} %slice_bitcast_fusion.3) | data formatting | bytes 1048576
  140.3 1.3 collective-permute-start.3
  141.6 4.3 %collective-permute-start.2 = (bf16[1,32,1,16,128]{1,3,4,2,0:T(8,128)(2,1)S(1)}, bf16[1,32,1,16,128]{1,3,4,2,0:T(8,128)(2,1)S(1)}, u32[]{:S(2)}, u32[]{:S(2)}) collective-permute-start(bf16[1,32,1,16,128]{1,3,4,2,0:T(8,128)(2,1)S(1)} %get-tuple-element.21), channel_id=1, source_target_pairs={{0,1},{1,2},{2,3},{3,4},{4,5},{5,6},{6,7},{7,8},{8,9},{9,10},{10,1... | collective-permute-start | bytes 393224 | tf_op jit(solution)/shard_map/ppermute | solution.py:12
  145.8 164.6 %all-reduce.3.cloned.1.call-done = f32[32,32,3,3,3]{1,0,4,3,2:T(8,128)} async-done(((f32[32,32,3,3,3]{1,0,4,3,2:T(8,128)}), f32[32,32,3,3,3]{1,0,4,3,2:T(8,128)}) %all-reduce.3.cloned.1.call-update) | async-done | bytes 110608 | tf_op jit(solution)/shard_map/psum | solution.py:69
  310.4 1.8 broadcast_multiply_fusion
  312.3 2.3 maximum_bitcast_fusion
  314.6 0.6 pad.7
  315.2 0.9 copy.146
  316.1 0.1 slice.140
  316.2 7.2 %select_convert_fusion = bf16[4,16,8,17,32]{4,2,3,1,0:T(8,128)(2,1)S(1)} fusion(pred[8,17]{0,1:T(8,128)(4,1)S(1)} %copy-done.11, bf16[32,32,3,3,3]{1,0,4,3,2:T(8,128)(2,1)S(1)} %copy-done, bf16[32,6,16,1,7,2]{0,4,5,2,1,3:T(8,128)(2,1)S(1)} %slice.140, bf16[32,6,16,1,8,17]{0,4,5,2,1,3:T(8,128)(2,1)S(1)} %copy.146), kind=kOutput, calls=%fused_computation.27 | convolution fusion | flops 464601088 | bytes 1534088 | tf_op jit(solution)/shard_map/conv_general_dilated | solution.py:21
  323.4 0.4 copy.147
  323.8 0.4 slice_bitcast_fusion.2
  324.2 2.9 copy.179
  (28 shorter events, 0.1 us)
Async XLA Ops:
  7.2 19.2 %copy-start = (bf16[32,32,3,3,3]{1,0,4,3,2:T(8,128)(2,1)S(1)}, bf16[32,32,3,3,3]{1,0,4,3,2:T(8,128)(2,1)}, u32[]{:S(2)}) copy-start(bf16[32,32,3,3,3]{1,0,4,3,2:T(8,128)(2,1)} %param.5) | copy-start | bytes 165892
  7.2 303.3 %all-reduce.3.cloned.1.call-start = ((), (), s32[]{:S(2)}) async-start(), calls=%async_computation | async-start | bytes 884736 | tf_op jit(solution)/shard_map/psum | solution.py:69
  8.7 8.9 %copy-start.3 = (bf16[1,32,4,16,128]{4,1,3,2,0:T(8,128)(2,1)}, bf16[1,32,4,16,128]{4,1,3,2,0:T(8,128)(2,1)S(1)}, u32[]{:S(2)}) copy-start(bf16[1,32,4,16,128]{4,1,3,2,0:T(8,128)(2,1)S(1)} %copy.135) | copy-start | bytes 1572868
  8.7 8.9 %collective-permute-start = (bf16[1,32,1,16,128]{4,1,3,2,0:T(8,128)(2,1)S(1)}, bf16[1,32,1,16,128]{4,1,3,2,0:T(8,128)(2,1)S(1)}, u32[]{:S(2)}, u32[]{:S(2)}) collective-permute-start(bf16[1,32,1,16,128]{4,1,3,2,0:T(8,128)(2,1)S(1)} %get-tuple-element.24), channel_id=1, source_target_pairs={{0,1},{1,2},{2,3},{3,4},{4,5},{5,6},{6,7},{7,8},{8,9},{9,10},{10,1... | collective-permute-start | bytes 393224 | tf_op jit(solution)/shard_map/ppermute | solution.py:12
  13.1 6.3 %collective-permute-start.1 = (bf16[1,32,1,16,128]{4,1,3,2,0:T(8,128)(2,1)S(1)}, bf16[1,32,1,16,128]{4,1,3,2,0:T(8,128)(2,1)S(1)}, u32[]{:S(2)}, u32[]{:S(2)}) collective-permute-start(bf16[1,32,1,16,128]{4,1,3,2,0:T(8,128)(2,1)S(1)} %get-tuple-element.23), channel_id=1, source_target_pairs={{1,0},{2,1},{3,2},{4,3},{5,4},{6,5},{7,6},{8,7},{9,8},{10,9},{11,1... | collective-permute-start | bytes 393224 | tf_op jit(solution)/shard_map/ppermute | solution.py:15
  17.6 7.7 %copy-start.8 = (bf16[1,32,1,16,128]{4,1,3,2,0:T(8,128)(2,1)}, bf16[1,32,1,16,128]{4,1,3,2,0:T(8,128)(2,1)S(1)}, u32[]{:S(2)}) copy-start(bf16[1,32,1,16,128]{4,1,3,2,0:T(8,128)(2,1)S(1)} %collective-permute-done) | copy-start | bytes 393220
  19.4 6.0 %copy-start.6 = (bf16[1,32,1,16,128]{4,1,3,2,0:T(8,128)(2,1)}, bf16[1,32,1,16,128]{4,1,3,2,0:T(8,128)(2,1)S(1)}, u32[]{:S(2)}) copy-start(bf16[1,32,1,16,128]{4,1,3,2,0:T(8,128)(2,1)S(1)} %collective-permute-done.1) | copy-start | bytes 393220
  25.4 1.0 copy-start.10
  25.4 1.0 copy-start.11
  40.4 1.3 copy-start.1
  41.7 4.2 %copy-start.4 = (bf16[1,32,4,16,128]{4,1,3,2,0:T(8,128)(2,1)S(1)}, bf16[1,32,4,16,128]{4,1,3,2,0:T(8,128)(2,1)}, u32[]{:S(2)}) copy-start(bf16[1,32,4,16,128]{4,1,3,2,0:T(8,128)(2,1)} %copy-done.3) | copy-start | bytes 1572868
  44.5 1.4 copy-start.9
  47.2 1.7 copy-start.2
  50.4 1.7 copy-start.7
  53.8 0.8 copy-start.5
  140.3 172.0 %collective-permute-start.3 = (bf16[1,32,1,16,128]{1,3,4,2,0:T(8,128)(2,1)S(1)}, bf16[1,32,1,16,128]{1,3,4,2,0:T(8,128)(2,1)S(1)}, u32[]{:S(2)}, u32[]{:S(2)}) collective-permute-start(bf16[1,32,1,16,128]{1,3,4,2,0:T(8,128)(2,1)S(1)} %get-tuple-element.22), channel_id=1, source_target_pairs={{1,0},{2,1},{3,2},{4,3},{5,4},{6,5},{7,6},{8,7},{9,8},{10,9},{11,1... | collective-permute-start | bytes 393224 | tf_op jit(solution)/shard_map/ppermute | solution.py:15
  141.6 170.7 %collective-permute-start.2 = (bf16[1,32,1,16,128]{1,3,4,2,0:T(8,128)(2,1)S(1)}, bf16[1,32,1,16,128]{1,3,4,2,0:T(8,128)(2,1)S(1)}, u32[]{:S(2)}, u32[]{:S(2)}) collective-permute-start(bf16[1,32,1,16,128]{1,3,4,2,0:T(8,128)(2,1)S(1)} %get-tuple-element.21), channel_id=1, source_target_pairs={{0,1},{1,2},{2,3},{3,4},{4,5},{5,6},{6,7},{7,8},{8,9},{9,10},{10,1... | collective-permute-start | bytes 393224 | tf_op jit(solution)/shard_map/ppermute | solution.py:12
Sparse Core Ops, SparseCore 0:
  54.7 255.6 all-reduce.2
where the time goes:
time: 334 us
  waiting for transfers between devices  165 us (49%)
  blocking collectives  81.2 us (24%)
  local copies, waits for them, and re-layouts  31 us (9%)
  matrix products  25.2 us (8%)
  between operations  14.4 us (4%)
  starting transfers between devices  11.3 us (3%)
  other arithmetic  5.9 us (2%)
    psum x1, waiting for transfers between devices, on_device(): lax.psum((local_kernel, local_offset), ('batch', 'slab'))  165 us
    psum x1, blocking collectives, on_device(): lax.psum((local_kernel, local_offset), ('batch', 'slab'))  81.2 us
    unnamed x31, local copies, waits for them, and re-layouts  18.4 us
    conv_general_dilated x2, matrix products, convolve_depth(): lax.conv_general_dilated(field, weights, (1, 1, 1), ((0, 0), (1, 1), (1,...  16.1 us
    dot_general x27, matrix products, kernel_terms(): jnp.einsum('nodhw,nidhw->oi', grad_pre, window, preferred_element_type=jn...  9.17 us
    ppermute x2, starting transfers between devices, padded_2(): lax.ppermute(lax.slice_in_dim(block, block.shape[dim] - width, None, axis...  8.66 us
  transfers between devices with their start and end apart: 5, of which 2 were waited for; matrix products, arithmetic and copies ran while one was open for 3% of the time, Pallas kernels for 0%

commit v1 on v0

--- a/solution.py
+++ b/solution.py
@@ -56,6 +56,10 @@
 
 
 def on_device(volume, kernel, offset, upstream):
+
+    def search_pairs_all_on_mesh(z_in, axis_id, row_axis):
+        return lax.psum(lax.psum(z_in, axis_id), row_axis)
+
     planes = volume.shape[2]
     flipped = jnp.transpose(jnp.flip(kernel, (2, 3, 4)), (1, 0, 2, 3, 4))
     bias = offset[None, :, None, None, None]
@@ -66,7 +70,9 @@
     grad_volume = convolve_depth(grad_haloed, flipped).astype(jnp.bfloat16)
     local_kernel = kernel_terms(haloed, grad_pre, planes).reshape(kernel.shape)
     local_offset = jnp.sum(grad_pre.astype(jnp.float32), axis=(0, 2, 3, 4))
-    summed_kernel, summed_offset = lax.psum((local_kernel, local_offset), ("batch", "slab"))
+    summed_kernel, summed_offset = search_pairs_all_on_mesh(
+        (local_kernel, local_offset), "batch", "slab"
+    )
     cells = (
         volume.shape[0]
         * planes

time: 334 us -> 302 us (0.904); the launches traced: 334 us -> 298 us
  waiting for transfers between devices: 165 us -> 135 us
  blocking collectives: 81.2 us -> 75.4 us
    psum x1 -> x2, waiting for transfers between devices: 165 us -> 134 us  [search_pairs_all_on_mesh(): return lax.psum(lax.psum(z_in, axis_id), row_axis)]
    psum x1 -> x2, blocking collectives: 81.2 us -> 75.4 us  [search_pairs_all_on_mesh(): return lax.psum(lax.psum(z_in, axis_id), row_axis)]
  transfers between devices with their start and end apart: 5 -> 6, of which waited for: 2 -> 2; matrix products, arithmetic and copies ran while one was open for 3% -> 12% of each run, Pallas kernels for 0% -> 0%
where the time goes in v1:
time: 302 us; the launch traced here: 298 us
  waiting for transfers between devices  135 us (45%)
  blocking collectives  75.4 us (25%)
  local copies, waits for them, and re-layouts  31 us (10%)
  matrix products  25.2 us (8%)
  between operations  14.4 us (5%)
  starting transfers between devices  11.6 us (4%)
  other arithmetic  5.82 us (2%)
    psum x2, waiting for transfers between devices, search_pairs_all_on_mesh(): return lax.psum(lax.psum(z_in, axis_id), row_axis)  134 us
    psum x2, blocking collectives, search_pairs_all_on_mesh(): return lax.psum(lax.psum(z_in, axis_id), row_axis)  75.4 us
    unnamed x31, local copies, waits for them, and re-layouts  17.2 us
    conv_general_dilated x2, matrix products, convolve_depth(): lax.conv_general_dilated(field, weights, (1, 1, 1), ((0, 0), (1, 1), (1,...  16.1 us
    dot_general x27, matrix products, kernel_terms(): jnp.einsum('nodhw,nidhw->oi', grad_pre, window, preferred_element_type=jn...  9.18 us
    ppermute x2, starting transfers between devices, padded_2(): lax.ppermute(lax.slice_in_dim(block, block.shape[dim] - width, None, axis...  8.92 us
  transfers between devices with their start and end apart: 6, of which 2 were waited for; matrix products, arithmetic and copies ran while one was open for 12% of the time, Pallas kernels for 0%

profile of v1, /device:TPU:1, one launch (start us, length us, event | category | flops | bytes accessed | tf_op | source)
XLA Modules:
  0.0 298.1 jit_solution(12646396375612248914)
XLA Ops:
  7.2 0.0 all-reduce.4.cloned.1.call-start
  7.2 1.4 copy.135
  8.7 4.4 %collective-permute-start = (bf16[1,32,1,16,128]{4,1,3,2,0:T(8,128)(2,1)S(1)}, bf16[1,32,1,16,128]{4,1,3,2,0:T(8,128)(2,1)S(1)}, u32[]{:S(2)}, u32[]{:S(2)}) collective-permute-start(bf16[1,32,1,16,128]{4,1,3,2,0:T(8,128)(2,1)S(1)} %get-tuple-element.24), channel_id=1, source_target_pairs={{0,1},{1,2},{2,3},{3,4},{4,5},{5,6},{6,7},{7,8},{8,9},{9,10},{10,1... | collective-permute-start | bytes 393224 | tf_op jit(solution)/shard_map/ppermute | solution.py:12
  13.1 1.3 collective-permute-start.1
  14.4 3.2 %copy.142 = bf16[1,32,4,16,128]{1,3,4,2,0:T(8,128)(2,1)S(1)} copy(bf16[1,32,4,16,128]{4,3,2,1,0:T(8,128)(2,1)} %param.7) | data formatting | bytes 1048576 | tf_op args[3]
  17.6 1.5 constant_dynamic-update-slice_fusion.1
  19.1 0.3 collective-permute-done.1
  19.4 3.4 %copy.207 = bf16[32,6,16,1,128]{0,2,4,1,3:T(8,128)(2,1)} copy(bf16[32,6,16,1,128]{4,0,2,1,3:T(8,128)(2,1)S(1)} %bitcast.363) | data formatting | bytes 1572864
  22.9 2.5 pad.5.clone
  25.4 0.9 copy.140
  26.3 0.1 slice.134
  26.4 8.8 %add_divide_fusion = (f32[4,16,8,17,32]{4,2,3,1,0:T(8,128)S(1)}, bf16[4,16,8,17,32]{4,2,3,1,0:T(8,128)(2,1)S(1)}, f32[4,16,8,17,32]{4,2,3,1,0:T(8,128)S(1)}) fusion(f32[32]{0:T(128)S(1)} %copy-done.10, pred[8,17]{0,1:T(8,128)(4,1)S(1)} %copy-done.11, bf16[32,32,3,3,3]{1,0,4,3,2:T(8,128)(2,1)S(1)} %copy-done, bf16[32,6,16,1,7,2]{0,4,5,2,1,3:T(8,128)(2,1)S(1)} %slice.134, ...), kind=kOutput, calls=%fused_computation.30 | convolution fusion | flops 466829312 | bytes 3762440 | tf_op jit(solution)/shard_map/conv_general_dilated | solution.py:21
  35.3 0.4 copy.141
  35.6 1.7 slice_bitcast_fusion.3
  37.3 0.8 copy.144
  38.1 1.0 copy.143
  39.1 1.2 convert_reduce_fusion
  40.3 1.3 fusion.138
  41.6 1.3 collective-permute-start.3
  42.9 4.5 %collective-permute-start.2 = (bf16[1,32,1,16,128]{1,3,4,2,0:T(8,128)(2,1)}, bf16[1,32,1,16,128]{1,3,4,2,0:T(8,128)(2,1)S(1)}, u32[]{:S(2)}, u32[]{:S(2)}) collective-permute-start(bf16[1,32,1,16,128]{1,3,4,2,0:T(8,128)(2,1)} %get-tuple-element.21), channel_id=1, source_target_pairs={{0,1},{1,2},{2,3},{3,4},{4,5},{5,6},{6,7},{7,8},{8,9},{9,10},{10,1... | collective-permute-start | bytes 393224 | tf_op jit(solution)/shard_map/ppermute | solution.py:12
  47.5 2.8 copy.148
  50.3 0.4 fusion.49
  50.7 0.3 fusion.48
  50.9 0.4 fusion.47
  51.3 0.4 fusion.46
  51.7 0.3 fusion.45
  52.0 0.4 fusion.44
  52.3 0.4 fusion.43
  52.7 0.3 fusion.42
  53.0 0.4 fusion.41
  53.3 0.4 fusion.40
  53.7 0.3 fusion.39
  54.0 0.4 fusion.38
  54.3 0.4 fusion.37
  54.7 0.5 fusion.36
  55.2 0.4 fusion.35
  55.5 0.4 fusion.34
  55.9 0.3 fusion.33
  56.2 0.4 fusion.32
  56.5 0.4 fusion.31
  56.9 0.3 fusion.30
  57.2 0.4 fusion.29
  57.5 0.4 fusion.28
  57.9 0.3 fusion.27
  58.2 0.4 fusion.26
  58.6 0.4 fusion.25
  58.9 0.3 fusion.24
  59.2 0.4 fusion.23
  59.6 0.8 copy-done.5
  60.4 0.0 all-reduce.6.cloned.1.call-start
  60.4 13.5 %psum.30 = f32[32]{0:T(128)S(1)} all-reduce(f32[32]{0:T(128)S(1)} %get-tuple-element.16), channel_id=1, replica_groups=mesh['batch'=8,'slab'=32] {'batch'}, use_global_device_ids=true, to_apply=%region_3.4 | all-reduce | flops 32 | bytes 256 | tf_op jit(solution)/shard_map/psum | solution.py:61
  73.9 61.9 %psum.31 = f32[32]{0:T(128)S(1)} all-reduce(f32[32]{0:T(128)S(1)} %psum.30), channel_id=1, replica_groups=mesh['batch'=8,'slab'=32] {'slab'}, use_global_device_ids=true, to_apply=%region_4.5 | all-reduce | flops 32 | bytes 256 | tf_op jit(solution)/shard_map/psum | solution.py:61
  135.8 0.5 broadcast_multiply_fusion.1
  136.3 4.0 %copy.178 = bf16[1,32,4,16,128]{4,3,2,1,0:T(8,128)(2,1)} copy(bf16[1,32,4,16,128]{1,3,4,2,0:T(8,128)(2,1)} %slice_bitcast_fusion.3) | data formatting | bytes 1048576
  140.3 2.3 maximum_bitcast_fusion
  142.7 0.6 pad.7
  143.3 0.9 copy.146
  144.2 0.1 slice.140
  144.3 7.2 %select_convert_fusion = bf16[4,16,8,17,32]{4,2,3,1,0:T(8,128)(2,1)S(1)} fusion(pred[8,17]{0,1:T(8,128)(4,1)S(1)} %copy-done.11, bf16[32,32,3,3,3]{1,0,4,3,2:T(8,128)(2,1)S(1)} %copy-done, bf16[32,6,16,1,7,2]{0,4,5,2,1,3:T(8,128)(2,1)S(1)} %slice.140, bf16[32,6,16,1,8,17]{0,4,5,2,1,3:T(8,128)(2,1)S(1)} %copy.146), kind=kOutput, calls=%fused_computation.27 | convolution fusion | flops 464601088 | bytes 1534088 | tf_op jit(solution)/shard_map/conv_general_dilated | solution.py:21
  151.5 0.4 copy.147
  151.9 0.4 slice_bitcast_fusion.2
  152.2 2.9 copy.179
  155.1 134.3 %all-reduce.6.cloned.1.call-done = f32[32,32,3,3,3]{1,0,4,3,2:T(8,128)} async-done(((f32[32,32,3,3,3]{1,0,4,3,2:T(8,128)}), f32[32,32,3,3,3]{1,0,4,3,2:T(8,128)}) %all-reduce.6.cloned.1.call-update) | async-done | bytes 110608 | tf_op jit(solution)/shard_map/psum | solution.py:61
  289.4 1.8 broadcast_multiply_fusion
  (32 shorter events, 0.2 us)
Async XLA Ops:
  7.2 19.2 %copy-start = (bf16[32,32,3,3,3]{1,0,4,3,2:T(8,128)(2,1)S(1)}, bf16[32,32,3,3,3]{1,0,4,3,2:T(8,128)(2,1)}, u32[]{:S(2)}) copy-start(bf16[32,32,3,3,3]{1,0,4,3,2:T(8,128)(2,1)} %param.5) | copy-start | bytes 165892
  7.2 133.1 %all-reduce.4.cloned.1.call-start = ((), (), s32[]{:S(2)}) async-start(), calls=%async_computation | async-start | bytes 884736 | tf_op jit(solution)/shard_map/psum | solution.py:61
  8.7 8.9 %copy-start.3 = (bf16[1,32,4,16,128]{4,1,3,2,0:T(8,128)(2,1)}, bf16[1,32,4,16,128]{4,1,3,2,0:T(8,128)(2,1)S(1)}, u32[]{:S(2)}) copy-start(bf16[1,32,4,16,128]{4,1,3,2,0:T(8,128)(2,1)S(1)} %copy.135) | copy-start | bytes 1572868
  8.7 8.9 %collective-permute-start = (bf16[1,32,1,16,128]{4,1,3,2,0:T(8,128)(2,1)S(1)}, bf16[1,32,1,16,128]{4,1,3,2,0:T(8,128)(2,1)S(1)}, u32[]{:S(2)}, u32[]{:S(2)}) collective-permute-start(bf16[1,32,1,16,128]{4,1,3,2,0:T(8,128)(2,1)S(1)} %get-tuple-element.24), channel_id=1, source_target_pairs={{0,1},{1,2},{2,3},{3,4},{4,5},{5,6},{6,7},{7,8},{8,9},{9,10},{10,1... | collective-permute-start | bytes 393224 | tf_op jit(solution)/shard_map/ppermute | solution.py:12
  13.1 6.3 %collective-permute-start.1 = (bf16[1,32,1,16,128]{4,1,3,2,0:T(8,128)(2,1)S(1)}, bf16[1,32,1,16,128]{4,1,3,2,0:T(8,128)(2,1)S(1)}, u32[]{:S(2)}, u32[]{:S(2)}) collective-permute-start(bf16[1,32,1,16,128]{4,1,3,2,0:T(8,128)(2,1)S(1)} %get-tuple-element.23), channel_id=1, source_target_pairs={{1,0},{2,1},{3,2},{4,3},{5,4},{6,5},{7,6},{8,7},{9,8},{10,9},{11,1... | collective-permute-start | bytes 393224 | tf_op jit(solution)/shard_map/ppermute | solution.py:15
  17.6 7.8 %copy-start.8 = (bf16[1,32,1,16,128]{4,1,3,2,0:T(8,128)(2,1)}, bf16[1,32,1,16,128]{4,1,3,2,0:T(8,128)(2,1)S(1)}, u32[]{:S(2)}) copy-start(bf16[1,32,1,16,128]{4,1,3,2,0:T(8,128)(2,1)S(1)} %collective-permute-done) | copy-start | bytes 393220
  19.4 6.0 %copy-start.6 = (bf16[1,32,1,16,128]{4,1,3,2,0:T(8,128)(2,1)}, bf16[1,32,1,16,128]{4,1,3,2,0:T(8,128)(2,1)S(1)}, u32[]{:S(2)}) copy-start(bf16[1,32,1,16,128]{4,1,3,2,0:T(8,128)(2,1)S(1)} %collective-permute-done.1) | copy-start | bytes 393220
  25.4 1.0 copy-start.10
  25.4 1.0 copy-start.11
  40.3 7.1 %copy-start.1 = (bf16[1,32,4,16,128]{1,3,4,2,0:T(8,128)(2,1)}, bf16[1,32,4,16,128]{1,3,4,2,0:T(8,128)(2,1)S(1)}, u32[]{:S(2)}) copy-start(bf16[1,32,4,16,128]{1,3,4,2,0:T(8,128)(2,1)S(1)} %get-tuple-element.17) | copy-start | bytes 1572868
  41.6 98.7 %collective-permute-start.3 = (bf16[1,32,1,16,128]{1,3,4,2,0:T(8,128)(2,1)}, bf16[1,32,1,16,128]{1,3,4,2,0:T(8,128)(2,1)S(1)}, u32[]{:S(2)}, u32[]{:S(2)}) collective-permute-start(bf16[1,32,1,16,128]{1,3,4,2,0:T(8,128)(2,1)} %get-tuple-element.22), channel_id=1, source_target_pairs={{1,0},{2,1},{3,2},{4,3},{5,4},{6,5},{7,6},{8,7},{9,8},{10,9},{11,1... | collective-permute-start | bytes 393224 | tf_op jit(solution)/shard_map/ppermute | solution.py:15
  42.9 97.4 %collective-permute-start.2 = (bf16[1,32,1,16,128]{1,3,4,2,0:T(8,128)(2,1)}, bf16[1,32,1,16,128]{1,3,4,2,0:T(8,128)(2,1)S(1)}, u32[]{:S(2)}, u32[]{:S(2)}) collective-permute-start(bf16[1,32,1,16,128]{1,3,4,2,0:T(8,128)(2,1)} %get-tuple-element.21), channel_id=1, source_target_pairs={{0,1},{1,2},{2,3},{3,4},{4,5},{5,6},{6,7},{7,8},{8,9},{9,10},{10,1... | collective-permute-start | bytes 393224 | tf_op jit(solution)/shard_map/ppermute | solution.py:12
  47.4 4.2 %copy-start.4 = (bf16[1,32,4,16,128]{4,1,3,2,0:T(8,128)(2,1)S(1)}, bf16[1,32,4,16,128]{4,1,3,2,0:T(8,128)(2,1)}, u32[]{:S(2)}) copy-start(bf16[1,32,4,16,128]{4,1,3,2,0:T(8,128)(2,1)} %copy-done.3) | copy-start | bytes 1572868
  50.3 1.4 copy-start.9
  53.0 1.7 copy-start.2
  56.2 1.7 copy-start.7
  59.5 0.8 copy-start.5
  60.4 229.1 %all-reduce.6.cloned.1.call-start = ((), (), s32[]{:S(2)}) async-start(), calls=%async_computation.1 | async-start | bytes 884736 | tf_op jit(solution)/shard_map/psum | solution.py:61
Sparse Core Ops, SparseCore 0:
  60.5 68.6 all-reduce.3
  140.4 148.9 all-reduce.5
